TPU v7x, 32 devices: a whole 2x2x4 slice. The times are simulated.
32 devices in a mesh: seq: 32 (over z, y, x, core), head: 1.
Axes of the slice: x: 2, y: 2, z: 4, core: 2. Of those that a mesh axis runs over, the one named last changes fastest.
Arguments:
- tree_queries: bfloat16 [4, 64, 128, 128], P(None, 'seq', 'head'), may hold values from -100 to 100
- tree_keys: bfloat16 [4, 64, 8, 128], P(None, 'seq', 'head'), may hold values from -12 to 12
- tree_values: bfloat16 [4, 64, 8, 128], P(None, 'seq', 'head'), may hold values from -6 to 6
- cache_keys: bfloat16 [4, 20480, 8, 128], P(None, 'seq', 'head'), may hold values from -6 to 6
- cache_values: bfloat16 [4, 20480, 8, 128], P(None, 'seq', 'head'), may hold values from -6 to 6
- out_weight: bfloat16 [16384, 16384], P('head', 'seq'), may hold values from -0.8984375 to 0.8984375
- context_lengths: int32 [4], replicated, may hold values from 2560 to 20472, as said below
- parents: int32 [4, 64], replicated, may hold values from -1 to 62, as said below
- accepted_nodes: int32 [4, 8], replicated, may hold values from 0 to 63, as said below
- accepted_count: int32 [4], replicated, may hold values from 1 to 8
Outputs:
- projected: bfloat16 [256, 16384], P('head', 'seq')
- keys_out: bfloat16 [4, 20480, 8, 128], P(None, 'seq', 'head')
- values_out: bfloat16 [4, 20480, 8, 128], P(None, 'seq', 'head')
Inputs may be any that keep to these rules, and one draw needn't show every extreme that they name: Request r's cache holds positions 0 to context_lengths[r] - 1; some request has the largest value in every draw. parents[r, 0] = -1 marks the root; for i >= 1, 0 <= parents[r, i] < i. `accepted_nodes`: each row lists distinct tree nodes in increasing order, the first being the root 0; entries j >= accepted_count[r] are not used.
All inputs are finite; a program needn't handle non-finite values.
Results may differ from a plain program's by a relative error of at most 0.0051.
Values may be sent and summed in bfloat16 or wider, within the bound.
A program may use at most 192 MiB of HBM per device.

v0:
```python
import math

import jax
import jax.numpy as jnp
from jax import lax
from jax.sharding import PartitionSpec as P

NEG = -1e30


def ancestors(parents):
    count_nodes = parents.shape[1]
    columns = jnp.arange(count_nodes, dtype=jnp.int32)
    linked = (parents[:, :, None] == columns[None, None, :]) | (
        columns[:, None] == columns[None, :]
    )[None]
    closure = linked.astype(jnp.float32)
    for rounds in range(max(count_nodes - 1, 1).bit_length()):
        closure = jnp.minimum(jnp.matmul(closure, closure, precision=lax.Precision.HIGHEST), 1.0)
    return closure


def partial_attention(queries, keys, values, allowed, scale_factor):
    scores = (
        jnp.einsum("rnhge,rphe->rnhgp", queries, keys, preferred_element_type=jnp.float32)
        * scale_factor
    )
    row_top = jnp.max(jnp.where(allowed, scores, NEG), axis=-1)
    weights = jnp.where(allowed, jnp.exp(scores - row_top[..., None]), 0.0)
    row_sum = jnp.sum(weights, axis=-1)
    numerator = jnp.einsum(
        "rnhgp,rphe->rnhge",
        weights.astype(jnp.bfloat16),
        values,
        preferred_element_type=jnp.float32,
    )
    return (row_top, row_sum, numerator)


def merge_parts(first, second):
    top_first, sum_first, acc_first = first
    top_second, sum_second, acc_second = second
    row_top = jnp.maximum(top_first, top_second)
    scale_first = jnp.exp(top_first - row_top)
    scale_second = jnp.exp(top_second - row_top)
    row_sum = sum_first * scale_first + sum_second * scale_second
    numerator = acc_first * scale_first[..., None] + acc_second * scale_second[..., None]
    return (row_top, row_sum, numerator)


def append_rows(cache_block, tree_all, choose, slot_map, written):
    picked = jnp.einsum(
        "rjn,rnhe->rjhe", choose, tree_all, preferred_element_type=jnp.float32
    ).astype(jnp.bfloat16)
    placed = jnp.einsum(
        "rjp,rjhe->rphe", slot_map, picked, preferred_element_type=jnp.float32
    ).astype(jnp.bfloat16)
    return jnp.where(written[:, :, None, None], placed, cache_block)


def on_device(
    tree_queries,
    tree_keys,
    tree_values,
    cache_keys,
    cache_values,
    out_weight,
    context_lengths,
    parents,
    accepted_nodes,
    accepted_count,
):
    requests, ctx_local, kv_local, head_dim = cache_keys.shape
    node_local, q_local = (tree_queries.shape[1], tree_queries.shape[2])
    group_size = q_local // kv_local
    path_len = accepted_nodes.shape[1]
    scale_factor = 1.0 / math.sqrt(head_dim)
    seq_index = lax.axis_index("seq")
    seq_count = lax.axis_size("seq")
    nodes_all = node_local * seq_count
    offset = seq_index * ctx_local
    grouped = tree_queries.reshape(requests, node_local, kv_local, group_size, head_dim)
    tree_all_k, tree_all_v = (
        lax.all_gather(tree_keys, "seq", axis=1, tiled=True),
        lax.all_gather(tree_values, "seq", axis=1, tiled=True),
    )
    closure = ancestors(parents)
    home_rows = lax.dynamic_slice_in_dim(closure, seq_index * node_local, node_local, 1)
    tree_state = partial_attention(
        grouped, tree_all_k, tree_all_v, home_rows[:, :, None, None, :] > 0.5, scale_factor
    )
    positions = offset + jnp.arange(ctx_local, dtype=jnp.int32)
    usable = (positions[None, :] < context_lengths[:, None])[:, None, None, None, :]
    everyone = lax.all_gather(grouped, "seq", axis=1, tiled=True)
    row_top, row_sum, numerator = partial_attention(
        everyone, cache_keys, cache_values, usable, scale_factor
    )
    highest = lax.pmax(row_top, "seq")
    factor = jnp.exp(row_top - highest)
    summed_acc, summed_sum = (
        lax.psum_scatter(numerator * factor[..., None], "seq", scatter_dimension=1, tiled=True),
        lax.psum_scatter(row_sum * factor, "seq", scatter_dimension=1, tiled=True),
    )
    home_top = lax.dynamic_slice_in_dim(highest, seq_index * node_local, node_local, 1)
    cache_state = (home_top, summed_sum, summed_acc)
    final_top, final_sum, final_acc = merge_parts(cache_state, tree_state)
    attention = (
        (final_acc / final_sum[..., None])
        .astype(jnp.bfloat16)
        .reshape(requests, node_local, q_local * head_dim)
    )
    partial_terms = jnp.einsum(
        "rnx,xd->rnd",
        lax.all_gather(attention, "seq", axis=1, tiled=True),
        out_weight,
        preferred_element_type=jnp.float32,
    )
    partial_terms = partial_terms.reshape(requests * nodes_all, out_weight.shape[1])
    projected = lax.psum_scatter(partial_terms, "head", scatter_dimension=0, tiled=True).astype(
        jnp.bfloat16
    )
    choose = (
        accepted_nodes[:, :, None] == jnp.arange(nodes_all, dtype=jnp.int32)[None, None, :]
    ).astype(jnp.bfloat16)
    steps_index = jnp.arange(path_len, dtype=jnp.int32)
    targets = context_lengths[:, None] + steps_index[None, :] - offset
    alive = steps_index[None, :] < accepted_count[:, None]
    slot_flags = (
        targets[:, :, None] == jnp.arange(ctx_local, dtype=jnp.int32)[None, None, :]
    ) & alive[:, :, None]
    slot_map = slot_flags.astype(jnp.bfloat16)
    written = jnp.sum(slot_flags.astype(jnp.float32), axis=1) > 0.5
    keys_out = append_rows(cache_keys, tree_all_k, choose, slot_map, written)
    values_out = append_rows(cache_values, tree_all_v, choose, slot_map, written)
    return (projected, keys_out, values_out)


def solution(mesh):
    in_specs = (
        P(None, "seq", "head", None),
        P(None, "seq", "head", None),
        P(None, "seq", "head", None),
        P(None, "seq", "head", None),
        P(None, "seq", "head", None),
        P("head", "seq"),
        P(),
        P(),
        P(),
        P(),
    )
    out_specs = (P("head", "seq"), P(None, "seq", "head", None), P(None, "seq", "head", None))
    return jax.shard_map(
        on_device, mesh=mesh, in_specs=in_specs, out_specs=out_specs, check_vma=False
    )
```

profile of v0, /device:TPU:0, one launch (start us, length us, event | category | flops | bytes accessed | tf_op | source)
XLA Modules:
  0.0 779.3 jit_solution(13525996675552482457)
XLA Ops:
  7.2 1.7 copy.96
  9.0 0.7 broadcast_compare_fusion.1
  9.7 81.9 %all-gather.3.cloned.1.call-done = bf16[4,64,8,16,128]{4,3,2,0,1:T(8,128)(2,1)} async-done(((bf16[4,2,8,16,128]{4,3,2,0,1:T(8,128)(2,1)}), bf16[4,64,8,16,128]{4,3,2,0,1:T(8,128)(2,1)}) %all-gather.3.cloned.1.call-update) | async-done | bytes 8388624 | tf_op jit(solution)/shard_map/all_gather | solution.py:94
  91.6 37.0 %fusion = (f32[4,64,8,16]{1,3,2,0:T(8,128)S(1)}, f32[4,8,640,64,16]{2,3,4,1,0:T(8,128)}) fusion(pred[4,640]{1,0:T(4,128)(4,1)S(1)} %broadcast_compare_fusion.1, bf16[4,64,8,16,128]{4,3,2,0,1:T(8,128)(2,1)} %all-gather.3.cloned.1.call-done, bf16[4,640,8,128,1]{3,2,1,0,4:T(8,128)(2,1)} %bitcast.81), kind=kOutput, calls=%fused_computation.2 | convolution fusion | flops 5431590912 | bytes 97651200 | tf_op jit(solution)/shard_map/rnhge,rphe->rnhgp/dot_general | solution.py:25
  128.7 1.3 copy.101
  130.1 29.4 %fusion.3 = f32[4,64,8,16]{1,3,2,0:T(8,128)S(1)} fusion(f32[4,8,640,64,16]{2,3,4,1,0:T(8,128)} %get-tuple-element.24, f32[4,64,8,16]{1,3,2,0:T(8,128)S(1)} %get-tuple-element.23, pred[4,640]{1,0:T(4,128)(4,1)S(1)} %broadcast_compare_fusion.1), kind=kLoop, calls=%fused_computation.5 | loop fusion | flops 83853312 | bytes 84150784 | tf_op jit(solution)/shard_map/reduce_sum | solution.py:30
  159.4 0.4 copy.113
  159.8 99.8 %all-reduce.4.cloned.1.call-done = f32[4,64,8,16]{3,2,1,0:T(8,128)} async-done(((f32[4,64,8,16]{3,2,1,0:T(8,128)}), f32[4,64,8,16]{3,2,1,0:T(8,128)}) %all-reduce.4.cloned.1.call-update) | async-done | bytes 131088 | tf_op jit(solution)/shard_map/pmax | solution.py:98
  259.6 1.4 fusion.70
  261.0 1.1 copy.114
  262.4 0.3 copy.102
  262.7 30.4 %bitcast_multiply_fusion = f32[4,64,8,16,128]{4,1,3,2,0:T(8,128)S(1)} fusion(f32[4,8,640,64,16]{2,3,4,1,0:T(8,128)} %get-tuple-element.24, f32[4,64,8,16]{1,3,2,0:T(8,128)S(1)} %get-tuple-element.23, pred[4,640]{1,0:T(4,128)(4,1)S(1)} %broadcast_compare_fusion.1, f32[4,64,8,16]{1,3,2,0:T(8,128)S(1)} %copy.102, bf16[4,640,8,128,1]{3,2,1,0,4:T(8,128)(2,1)} %bitcast.86), kind=kOutput, calls=%fused_computation.11 | convolution fusion | flops 5456789504 | bytes 106170880 | tf_op jit(solution)/shard_map/rnhgp,rphe->rnhge/dot_general | solution.py:31
  293.1 11.5 %copy.103 = f32[4,64,8,16,128]{4,3,1,2,0:T(8,128)} copy(f32[4,64,8,16,128]{4,1,3,2,0:T(8,128)S(1)} %bitcast_multiply_fusion) | data formatting | bytes 33554432 | tf_op jit(solution)/shard_map/mul | solution.py:101
  304.8 0.6 copy-done.2
  305.7 0.3 convolution_minimum_fusion.3
  305.9 0.3 convolution_minimum_fusion.2
  306.2 0.3 convolution_minimum_fusion.1
  307.0 41.1 %all_gather.13 = bf16[4,64,8,128]{3,2,0,1:T(8,128)(2,1)S(1)} all-gather(bf16[4,2,8,128]{3,2,0,1:T(8,128)(2,1)S(1)} %copy.104), channel_id=1, replica_groups=mesh['seq'=32,'head'=1] {'seq'}, dimensions={1}, use_global_device_ids=true | all-gather | bytes 540672 | tf_op jit(solution)/shard_map/all_gather | solution.py:84
  348.1 0.5 select_reduce_fusion
  348.6 0.5 fusion.33
  349.0 38.4 %all_gather.14 = bf16[4,64,8,128]{3,2,0,1:T(8,128)(2,1)S(1)} all-gather(bf16[4,2,8,128]{3,2,0,1:T(8,128)(2,1)S(1)} %copy.109), channel_id=1, replica_groups=mesh['seq'=32,'head'=1] {'seq'}, dimensions={1}, use_global_device_ids=true | all-gather | bytes 540672 | tf_op jit(solution)/shard_map/all_gather | solution.py:85
  387.4 9.4 %reduce-scatter.5.cloned.1.call-done = f32[4,2,8,16]{3,2,0,1:T(8,128)} async-done(((f32[4,64,8,16]{3,2,0,1:T(8,128)}), f32[4,2,8,16]{3,2,0,1:T(8,128)}) %reduce-scatter.5.cloned.1.call-update) | async-done | bytes 4112 | tf_op jit(solution)/shard_map/reduce_scatter | solution.py:102
  396.9 0.8 fusion.54
  397.7 279.4 %all-reduce.6.cloned.1.call-done = f32[4,64,8,16,128]{4,3,1,2,0:T(8,128)} async-done(((f32[4,64,8,16,128]{4,3,1,2,0:T(8,128)}), f32[4,64,8,16,128]{4,3,1,2,0:T(8,128)}) %all-reduce.6.cloned.1.call-update) | async-done | bytes 16777232
  677.2 1.7 fusion.21
  678.9 0.8 reshape.116
  680.0 6.0 copy_select_fusion.1
  686.0 8.3 %copy.125 = bf16[4,640,8,128]{3,2,1,0:T(8,128)(2,1)} copy(bf16[4,640,8,128]{3,1,2,0:T(8,128)(2,1)} %copy_select_fusion.1) | data formatting | bytes 10485760
  694.2 6.0 copy_select_fusion
  700.3 8.2 %copy.126 = bf16[4,640,8,128]{3,2,1,0:T(8,128)(2,1)} copy(bf16[4,640,8,128]{3,1,2,0:T(8,128)(2,1)} %copy_select_fusion) | data formatting | bytes 10485760
  708.5 49.3 %all-gather.5.cloned.1.call-done = bf16[4,64,16384]{2,0,1:T(4,128)(2,1)} async-done(((bf16[4,2,16384]{2,0,1:T(4,128)(2,1)}), bf16[4,64,16384]{2,0,1:T(4,128)(2,1)}) %all-gather.5.cloned.1.call-update) | async-done | bytes 8388624 | tf_op jit(solution)/shard_map/all_gather | solution.py:114
  757.8 14.9 %fusion.22 = bf16[4,64,512]{2,1,0:T(8,128)(2,1)} fusion(bf16[16384,512]{1,0:T(8,128)(2,1)} %param.15, bf16[4,64,16384]{2,0,1:T(4,128)(2,1)} %all-gather.5.cloned.1.call-done), kind=kOutput, calls=%fused_computation.26 | convolution fusion | flops 4295098368 | bytes 25427968 | tf_op jit(solution)/shard_map/rnx,xd->rnd/dot_general | solution.py:112
  (41 shorter events, 1.7 us)
Async XLA Ops:
  7.2 84.5 %all-gather.3.cloned.1.call-start = ((), (), s32[]{:S(2)}) async-start(), calls=%async_computation.1 | async-start | bytes 8650752 | tf_op jit(solution)/shard_map/all_gather | solution.py:94
  8.9 250.7 %all-reduce.4.cloned.1.call-start = ((), (), s32[]{:S(2)}) async-start(), calls=%async_computation.2 | async-start | bytes 2097152 | tf_op jit(solution)/shard_map/pmax | solution.py:98
  130.0 266.8 %reduce-scatter.5.cloned.1.call-start = ((), (), s32[]{:S(2)}) async-start(), calls=%async_computation.3 | async-start | bytes 1081344 | tf_op jit(solution)/shard_map/reduce_scatter | solution.py:102
  130.1 129.5 %copy-start = (f32[4,64,8,16]{3,2,1,0:T(8,128)S(1)}, f32[4,64,8,16]{3,2,1,0:T(8,128)}, u32[]{:S(2)}) copy-start(f32[4,64,8,16]{3,2,1,0:T(8,128)} %copy.101) | copy-start | bytes 393220
  262.2 415.0 %all-reduce.6.cloned.1.call-start = ((), (), s32[]{:S(2)}) async-start(), calls=%async_computation.5 | async-start | bytes 33554432
  304.6 0.7 copy-start.2
  304.6 0.7 copy-start.3
  304.6 0.8 copy-start.5
  304.6 43.4 %copy-start.1 = (bf16[4,2,128,128]{3,2,1,0:T(8,128)(2,1)S(1)}, bf16[4,2,128,128]{3,2,1,0:T(8,128)(2,1)}, u32[]{:S(2)}) copy-start(bf16[4,2,128,128]{3,2,1,0:T(8,128)(2,1)} %param.10) | copy-start | bytes 786436
  304.7 375.1 %copy-start.7 = (s32[4]{0:T(128)S(1)}, s32[4]{0:T(128)}, u32[]{:S(2)}) copy-start(s32[4]{0:T(128)} %param.19) | copy-start | bytes 52
  304.7 375.1 %copy-start.4 = (s32[4]{0:T(128)S(1)}, s32[4]{0:T(128)}, u32[]{:S(2)}) copy-start(s32[4]{0:T(128)} %param.16) | copy-start | bytes 52
  304.7 375.3 %copy-start.6 = (s32[4,8]{1,0:T(4,128)S(1)}, s32[4,8]{1,0:T(4,128)}, u32[]{:S(2)}) copy-start(s32[4,8]{1,0:T(4,128)} %param.18) | copy-start | bytes 388
  304.7 453.1 %all-gather.5.cloned.1.call-start = ((), (), s32[]{:S(2)}) async-start(), calls=%async_computation.4 | async-start | bytes 8650752 | tf_op jit(solution)/shard_map/all_gather | solution.py:114
Sparse Core Ops, SparseCore 0:
  11.4 80.1 all-gather.2
  130.1 129.4 all-reduce.3
  262.5 134.2 reduce-scatter.4
  402.8 274.3 all-reduce.5
  680.4 77.3 all-gather.4
where the time goes:
time: 780 us; the launch traced here: 779 us
  waiting for transfers between devices  520 us (67%)
  matrix products  98.1 us (13%)
  blocking collectives  79.5 us (10%)
  local copies, waits for them, and re-layouts  34.4 us (4%)
  other arithmetic  33 us (4%)
  between operations  14 us (2%)
    unnamed x6, waiting for transfers between devices  280 us
    pmax x1, waiting for transfers between devices, on_device(): highest = lax.pmax(row_top, 'seq')  99.8 us
    all_gather x1, waiting for transfers between devices, on_device(): everyone = lax.all_gather(grouped, 'seq', axis=1, tiled=True)  81.9 us
    all_gather x1, waiting for transfers between devices, on_device(): lax.all_gather(attention, 'seq', axis=1, tiled=True)  49.3 us
    all_gather x1, blocking collectives, on_device(): lax.all_gather(tree_keys, 'seq', axis=1, tiled=True)  41.1 us
    all_gather x1, blocking collectives, on_device(): lax.all_gather(tree_values, 'seq', axis=1, tiled=True)  38.4 us
    dot_general x2, matrix products, partial_attention(): jnp.einsum('rnhge,rphe->rnhgp', queries, keys, preferred_element_type=jnp...  37.5 us
    dot_general x2, matrix products, partial_attention(): jnp.einsum('rnhgp,rphe->rnhge', weights.astype(jnp.bfloat16), values, pre...  32.1 us
  transfers between devices with their start and end apart: 5, of which 5 were waited for; matrix products, arithmetic and copies ran while one was open for 13% of the time, Pallas kernels for 0%

commit v1 on v0

--- a/solution.py
+++ b/solution.py
@@ -1,8 +1,11 @@
+import functools
 import math
 
 import jax
 import jax.numpy as jnp
 from jax import lax
+from jax.experimental import pallas as pl
+from jax.experimental.pallas import tpu as pltpu
 from jax.sharding import PartitionSpec as P
 
 NEG = -1e30
@@ -58,7 +61,7 @@
     return jnp.where(written[:, :, None, None], placed, cache_block)
 
 
-def on_device(
+def on_device_plain(
     tree_queries,
     tree_keys,
     tree_values,
@@ -135,6 +138,461 @@
     return (projected, keys_out, values_out)
 
 
+MESH = pl.DeviceIdType.MESH
+LOG2E = math.log2(math.e)
+
+
+def bit_of(me, bit):
+    return (me // (1 << bit)) % 2
+
+
+def partner_of(me, bit):
+    return me + (1 - 2 * bit_of(me, bit)) * (1 << bit)
+
+
+def greet(me, levels):
+    barrier = pltpu.get_barrier_semaphore()
+    for bit in range(levels):
+        pl.semaphore_signal(
+            barrier, inc=1, device_id={"seq": partner_of(me, bit)}, device_id_type=MESH
+        )
+    pl.semaphore_wait(barrier, levels)
+
+
+def gather_orders(levels):
+    high = list(range(levels - 1, 2, -1))
+    return (high + [1, 2, 0], high + [2, 1, 0])
+
+
+def gather_kernel(levels, chunks, mine, out, own_sem, send_sem, recv_sem):
+    me = lax.axis_index("seq")
+    orders = gather_orders(levels)
+    own = [bit_of(me, bit) for bit in range(levels)]
+    greet(me, levels)
+
+    def copy(c, p, half):
+        done = orders[half][:p]
+        where = tuple(
+            slice(None) if bit in done else own[bit] for bit in range(levels - 1, -1, -1)
+        )
+        place = out.at[(c,) + where + (half,)]
+        return pltpu.make_async_remote_copy(
+            src_ref=mine.at[c, half] if p == 0 else place,
+            dst_ref=place,
+            send_sem=send_sem.at[c, p, half],
+            recv_sem=recv_sem.at[c, p, half],
+            device_id={"seq": partner_of(me, orders[half][p])},
+            device_id_type=MESH,
+        )
+
+    mine_bits = tuple(own[bit] for bit in range(levels - 1, -1, -1))
+    locals_ = [
+        pltpu.make_async_copy(mine.at[c], out.at[(c,) + mine_bits], own_sem.at[c])
+        for c in range(chunks)
+    ]
+    copies = {}
+    for c in range(chunks):
+        for half in range(2):
+            copies[c, 0, half] = copy(c, 0, half)
+            copies[c, 0, half].start()
+    for c in range(chunks):
+        locals_[c].start()
+    for step in range(chunks + levels):
+        for p in range(levels, 0, -1):
+            c = step - p
+            if not 0 <= c < chunks:
+                continue
+            if p == 1:
+                locals_[c].wait()
+            for half in range(2):
+                copies[c, p - 1, half].wait_recv()
+                if p < levels:
+                    copies[c, p, half] = copy(c, p, half)
+                    copies[c, p, half].start()
+    for pending in copies.values():
+        pending.wait_send()
+
+
+def gather(block, count, collective_id):
+    chunks = block.shape[0]
+    levels = count.bit_length() - 1
+    out = pl.pallas_call(
+        functools.partial(gather_kernel, levels, chunks),
+        out_shape=jax.ShapeDtypeStruct(
+            (chunks,) + (2,) * levels + block.shape[1:], block.dtype
+        ),
+        in_specs=[pl.BlockSpec(memory_space=pl.ANY)],
+        out_specs=pl.BlockSpec(memory_space=pl.ANY),
+        scratch_shapes=[
+            pltpu.SemaphoreType.DMA((chunks,)),
+            pltpu.SemaphoreType.DMA((chunks, levels, 2)),
+            pltpu.SemaphoreType.DMA((chunks, levels, 2)),
+        ],
+        compiler_params=pltpu.CompilerParams(
+            collective_id=collective_id, has_side_effects=True
+        ),
+    )(block)
+    return out.reshape((chunks, count) + block.shape[1:])
+
+
+def scatter_kernel(levels, chunks, acc, logs, out, work, work_s, load_sem, send_sem, recv_sem, *recv):
+    me = lax.axis_index("seq")
+    orders = tuple(order[::-1] for order in gather_orders(levels))
+    own = [bit_of(me, bit) for bit in range(levels)]
+    held, held_s = recv[:levels], recv[levels:]
+    rows = out.shape[2]
+    loads = []
+    for c in range(chunks):
+        loads.append(pltpu.make_async_copy(acc.at[c], work.at[c], load_sem.at[0, c]))
+        loads.append(pltpu.make_async_copy(logs.at[c], work_s.at[c], load_sem.at[1, c]))
+    for load in loads:
+        load.start()
+    greet(me, levels)
+
+    def send(c, p, half):
+        bit_now = orders[half][p]
+        done = orders[half][:p]
+        where = []
+        for bit in range(levels - 1, -1, -1):
+            if bit in done:
+                where.append(own[bit])
+            elif bit == bit_now:
+                where.append(1 - own[bit])
+            else:
+                where.append(slice(None))
+        place = (c,) + tuple(where) + (half,)
+        made = []
+        for kind, (source, target) in enumerate(((work, held[p]), (work_s, held_s[p]))):
+            made.append(
+                pltpu.make_async_remote_copy(
+                    src_ref=source.at[place],
+                    dst_ref=target.at[c, half],
+                    send_sem=send_sem.at[kind, c, p, half],
+                    recv_sem=recv_sem.at[kind, c, p, half],
+                    device_id={"seq": partner_of(me, bit_now)},
+                    device_id_type=MESH,
+                )
+            )
+        for one in made:
+            one.start()
+        return made
+
+    row_id = lax.broadcasted_iota(jnp.int32, (rows, rows), 0)
+    column_id = lax.broadcasted_iota(jnp.int32, (rows, rows), 1)
+    diagonal = row_id == column_id
+
+    def merge(c, p, half):
+        done = orders[half][: p + 1]
+        free = [bit for bit in range(levels - 1, -1, -1) if bit not in done]
+        last = p == levels - 1
+
+        def body(k, carry):
+            place, there, rank = [], [], len(free)
+            for bit in range(levels - 1, -1, -1):
+                if bit in done:
+                    place.append(own[bit])
+                else:
+                    rank -= 1
+                    digit = (k // (1 << rank)) % 2
+                    place.append(digit)
+                    there.append(digit)
+            at_work = (c,) + tuple(place) + (half,)
+            at_held = (c, half) + tuple(there)
+            log_a, log_b = work_s[at_work], held_s[p][at_held]
+            top = jnp.maximum(log_a, log_b)
+            part_a, part_b = jnp.exp2(log_a - top), jnp.exp2(log_b - top)
+            total = part_a + part_b
+            share = jnp.sum(
+                jnp.where(diagonal, part_a / total, 0.0), axis=1, keepdims=True
+            )
+            merged = (
+                work[at_work].astype(jnp.float32) * share
+                + held[p][at_held].astype(jnp.float32) * (1.0 - share)
+            ).astype(jnp.bfloat16)
+            if last:
+                out[c, half] = merged
+            else:
+                work[at_work] = merged
+                work_s[at_work] = top + jnp.log2(total)
+            return carry
+
+        if free:
+            lax.fori_loop(0, 1 << len(free), body, 0)
+        else:
+            body(0, 0)
+
+    copies = {}
+    for c in range(chunks):
+        loads[2 * c].wait()
+        loads[2 * c + 1].wait()
+        for half in range(2):
+            copies[c, 0, half] = send(c, 0, half)
+    for step in range(chunks + levels):
+        for p in range(levels, 0, -1):
+            c = step - p
+            if not 0 <= c < chunks:
+                continue
+            for half in range(2):
+                for one in copies[c, p - 1, half]:
+                    one.wait_recv()
+                merge(c, p - 1, half)
+                if p < levels:
+                    copies[c, p, half] = send(c, p, half)
+    for pair in copies.values():
+        for one in pair:
+            one.wait_send()
+
+
+def scatter_merge(acc, logs, count, collective_id):
+    chunks, _, _, rows, width = acc.shape
+    levels = count.bit_length() - 1
+    bits = (2,) * levels
+    held = [pltpu.VMEM((chunks, 2) + bits[: levels - 1 - p] + (rows, width), jnp.bfloat16) for p in range(levels)]
+    held_s = [pltpu.VMEM((chunks, 2) + bits[: levels - 1 - p] + (1, rows), jnp.float32) for p in range(levels)]
+    return pl.pallas_call(
+        functools.partial(scatter_kernel, levels, chunks),
+        out_shape=jax.ShapeDtypeStruct((chunks, 2, rows, width), jnp.bfloat16),
+        in_specs=[pl.BlockSpec(memory_space=pl.ANY)] * 2,
+        out_specs=pl.BlockSpec(memory_space=pltpu.VMEM),
+        scratch_shapes=[
+            pltpu.VMEM((chunks,) + bits + (2, rows, width), jnp.bfloat16),
+            pltpu.VMEM((chunks,) + bits + (2, 1, rows), jnp.float32),
+            pltpu.SemaphoreType.DMA((2, chunks)),
+            pltpu.SemaphoreType.DMA((2, chunks, levels, 2)),
+            pltpu.SemaphoreType.DMA((2, chunks, levels, 2)),
+        ]
+        + held
+        + held_s,
+        compiler_params=pltpu.CompilerParams(
+            collective_id=collective_id, has_side_effects=True, vmem_limit_bytes=48 * 2**20
+        ),
+    )(acc.reshape((chunks,) + bits + (2, rows, width)), logs.reshape((chunks,) + bits + (2, 1, rows)))
+
+
+def attend_kernel(
+    scale, where, lengths, accepted, count,
+    q, k, v, tree_k, tree_v, own_k, own_v, own_bias,
+    acc, logs, k_out, v_out, k_wide, v_wide,
+):
+    r, h = pl.program_id(0), pl.program_id(1)
+    ctx, kv, width = k.shape[1:]
+    nodes, group = q.shape[1:3]
+    me, offset = where[0], where[1]
+
+    @pl.when(h == 0)
+    def _():
+        for cache, wide, fresh, target in ((k, k_wide, tree_k, k_out), (v, v_wide, tree_v, v_out)):
+            wide[...] = cache[0].astype(jnp.float32).reshape(ctx * kv, width)
+            target[...] = cache[...]
+            for j in range(accepted.shape[1]):
+                slot = lengths[r] + j - offset
+
+                @pl.when((j < count[r]) & (slot >= 0) & (slot < ctx))
+                def _():
+                    target[0, slot] = fresh[0, accepted[r, j]]
+
+    keys = k_wide[pl.ds(h, ctx, stride=kv), :].astype(jnp.bfloat16)
+    values = v_wide[pl.ds(h, ctx, stride=kv), :].astype(jnp.bfloat16)
+    position = offset + lax.broadcasted_iota(jnp.int32, (1, ctx), 1)
+    bias = jnp.where(position < lengths[r], 0.0, NEG)
+    queries = q[0].reshape(nodes * group, width)
+    tile = 2 * width
+    diagonal = lax.broadcasted_iota(jnp.int32, (width, width), 0) == lax.broadcasted_iota(
+        jnp.int32, (width, width), 1
+    )
+
+    def block(rows, key, value, bias):
+        scores = lax.dot_general(
+            rows, key, (((1,), (1,)), ((), ())), preferred_element_type=jnp.float32
+        )
+        scores = scores * (scale * LOG2E) + bias
+        top = jnp.max(scores, axis=1, keepdims=True)
+        weights = jnp.exp2(scores - top)
+        total = jnp.sum(weights, axis=1, keepdims=True)
+        number = jnp.dot(weights.astype(jnp.bfloat16), value, preferred_element_type=jnp.float32)
+        return top, total, number
+
+    def store(start, top, total, number):
+        acc[0, start : start + tile] = (number / total).astype(jnp.bfloat16)
+        lines = top + jnp.log2(total)
+        for part in range(tile // width):
+            line = jnp.sum(
+                jnp.where(diagonal, lines[part * width : (part + 1) * width], 0.0),
+                axis=0,
+                keepdims=True,
+            )
+            at = start // width + part
+            logs[0, at : at + 1, :] = line
+
+    has_tree = (r * kv + h) == me
+    for start in range(0, nodes * group, tile):
+        rows = queries[start : start + tile]
+        top, total, number = block(rows, keys, values, bias)
+        store(start, top, total, number)
+
+    @pl.when(has_tree)
+    def _():
+        for start in range(0, nodes * group, tile):
+            rows = queries[start : start + tile]
+            top, total, number = block(rows, keys, values, bias)
+            t_top, t_total, t_number = block(
+                rows, own_k[...], own_v[...], own_bias[start : start + tile]
+            )
+            high = jnp.maximum(top, t_top)
+            fa, fb = jnp.exp2(top - high), jnp.exp2(t_top - high)
+            store(start, high, total * fa + t_total * fb, number * fa + t_number * fb)
+
+
+def attend(scale, where, lengths, accepted, count, q_all, k, v, tree_k, tree_v, own_k, own_v, own_bias):
+    requests, ctx, kv, width = k.shape
+    nodes = q_all.shape[1]
+    group = own_bias.shape[0] // nodes
+    rows = nodes * group
+    whole = pl.BlockSpec(memory_space=pltpu.VMEM)
+    by_request = lambda r, h, *_: (r, 0, 0, 0)
+    cache_spec = pl.BlockSpec((1, ctx, kv, width), by_request)
+    tree_spec = pl.BlockSpec((1, nodes, kv, width), by_request)
+    work = requests * kv * rows * ctx
+    return pl.pallas_call(
+        functools.partial(attend_kernel, scale),
+        grid_spec=pltpu.PrefetchScalarGridSpec(
+            num_scalar_prefetch=4,
+            grid=(requests, kv),
+            in_specs=[
+                pl.BlockSpec((1, nodes, group, width), lambda r, h, *_: (r, 0, h, 0)),
+                cache_spec, cache_spec, tree_spec, tree_spec, whole, whole, whole,
+            ],
+            out_specs=[
+                pl.BlockSpec((1, rows, width), lambda r, h, *_: (r, h, 0)),
+                pl.BlockSpec((1, rows // width, width), lambda r, h, *_: (r, h, 0)),
+                cache_spec, cache_spec,
+            ],
+            scratch_shapes=[pltpu.VMEM((ctx * kv, width), jnp.float32)] * 2,
+        ),
+        out_shape=[
+            jax.ShapeDtypeStruct((requests, kv * rows, width), jnp.bfloat16),
+            jax.ShapeDtypeStruct((requests, kv * rows // width, width), jnp.float32),
+            jax.ShapeDtypeStruct(k.shape, k.dtype),
+            jax.ShapeDtypeStruct(v.shape, v.dtype),
+        ],
+        compiler_params=pltpu.CompilerParams(vmem_limit_bytes=48 * 2**20),
+        cost_estimate=pl.CostEstimate(
+            flops=4 * work * width, bytes_accessed=4 * k.size * 2, transcendentals=work
+        ),
+    )(where, lengths, accepted, count, q_all, k, v, tree_k, tree_v, own_k, own_v, own_bias)
+
+
+def project_kernel(a, w, out, total):
+    step = pl.program_id(0)
+
+    @pl.when(step == 0)
+    def _():
+        total[...] = jnp.zeros_like(total)
+
+    requests, _, parts, group, some, width = a.shape
+    rows = requests * parts * some
+    term = None
+    for g in range(0, group, 2):
+        left = jnp.concatenate(
+            [a[:, 0, :, g + i].reshape(rows, width) for i in range(2)], axis=1
+        )
+        now = jnp.dot(
+            left, w[g * width : (g + 2) * width, :], preferred_element_type=jnp.float32
+        )
+        term = now if term is None else term + now
+    total[...] += term
+
+    @pl.when(step == pl.num_programs(0) - 1)
+    def _():
+        out[...] = total[...].astype(out.dtype)
+
+
+def project(attention, weight):
+    requests, kv, parts, group, some, width = attention.shape
+    rows = requests * parts * some
+    columns = weight.shape[1]
+    return pl.pallas_call(
+        project_kernel,
+        grid=(kv,),
+        in_specs=[
+            pl.BlockSpec((requests, 1, parts, group, some, width), lambda h: (0, h, 0, 0, 0, 0)),
+            pl.BlockSpec((group * width, columns), lambda h: (h, 0)),
+        ],
+        out_specs=pl.BlockSpec((rows, columns), lambda h: (0, 0)),
+        out_shape=jax.ShapeDtypeStruct((rows, columns), jnp.bfloat16),
+        scratch_shapes=[pltpu.VMEM((rows, columns), jnp.float32)],
+        compiler_params=pltpu.CompilerParams(vmem_limit_bytes=40 * 2**20),
+    )(attention, weight)
+
+
+def on_device(
+    tree_queries,
+    tree_keys,
+    tree_values,
+    cache_keys,
+    cache_values,
+    out_weight,
+    context_lengths,
+    parents,
+    accepted_nodes,
+    accepted_count,
+):
+    requests, ctx, kv, width = cache_keys.shape
+    node_local, heads = tree_queries.shape[1:3]
+    group = heads // kv
+    count = lax.axis_size("seq")
+    nodes = node_local * count
+    part = kv * nodes // count
+    me = lax.axis_index("seq")
+    sent = jnp.concatenate([tree_queries, tree_keys, tree_values], axis=2)
+    closure = ancestors(parents)
+    everyone = gather(sent, count, 1).reshape(requests, nodes, heads + 2 * kv, width)
+    tree_k = everyone[:, :, heads : heads + kv]
+    tree_v = everyone[:, :, heads + kv :]
+    pair = lax.rem(me, requests * kv)
+    own_request, own_head = pair // kv, lax.rem(pair, kv)
+    own_k = lax.dynamic_slice(tree_k, (own_request, 0, own_head, 0), (1, nodes, 1, width))
+    own_v = lax.dynamic_slice(tree_v, (own_request, 0, own_head, 0), (1, nodes, 1, width))
+    own_reach = lax.dynamic_index_in_dim(closure, own_request, 0, keepdims=False)
+    own_bias = jnp.repeat(jnp.where(own_reach > 0.5, 0.0, NEG), group, axis=0)
+    acc, logs, keys_out, values_out = attend(
+        1.0 / math.sqrt(width),
+        jnp.stack([me, me * ctx]).astype(jnp.int32),
+        context_lengths, accepted_nodes, accepted_count,
+        everyone, cache_keys, cache_values, tree_k, tree_v,
+        own_k.reshape(nodes, width), own_v.reshape(nodes, width), own_bias,
+    )
+    half_rows = part * group // 2
+    home = scatter_merge(
+        acc.reshape(requests, count, 2, half_rows, width),
+        logs.reshape(requests, count, 2, 1, half_rows),
+        count,
+        2,
+    )
+    home = home.reshape(requests, part, group, width).swapaxes(1, 2)
+    attention = gather(home.reshape(requests, 2, half_rows, width), count, 3)
+    attention = attention.reshape(requests, kv, count // kv, group, part, width)
+    return (project(attention, out_weight), keys_out, values_out)
+
+
+def fits(mesh, args):
+    queries, keys = args[0], args[3]
+    count, split = mesh.shape["seq"], mesh.shape["head"]
+    requests, nodes, heads, width = queries.shape
+    kv = keys.shape[2]
+    rows = nodes * heads // count
+    return (
+        split == 1
+        and count >= 8
+        and count & (count - 1) == 0
+        and count % kv == 0
+        and count >= requests * kv
+        and nodes * kv // count % 16 == 0
+        and nodes == 2 * count
+        and rows == 2 * width
+    )
+
+
 def solution(mesh):
     in_specs = (
         P(None, "seq", "head", None),
@@ -149,6 +607,11 @@
         P(),
     )
     out_specs = (P("head", "seq"), P(None, "seq", "head", None), P(None, "seq", "head", None))
-    return jax.shard_map(
-        on_device, mesh=mesh, in_specs=in_specs, out_specs=out_specs, check_vma=False
-    )
+
+    def run(*args):
+        body = on_device if fits(mesh, args) else on_device_plain
+        return jax.shard_map(
+            body, mesh=mesh, in_specs=in_specs, out_specs=out_specs, check_vma=False
+        )(*args)
+
+    return run

time: 780 us -> 285 us (0.37)
  waiting for transfers between devices: 520 us -> 0 us
  Pallas kernels: 0 us -> 272 us
  matrix products: 98.1 us -> 2.28 us
  blocking collectives: 79.5 us -> 0 us
  other arithmetic: 33 us -> 1.82 us
  local copies, waits for them, and re-layouts: 34.4 us -> 5.57 us
  between operations: 14 us -> 0.84 us
    unnamed x6 -> x0, waiting for transfers between devices: 280 us -> none
    pallas_call x0 -> x5, Pallas kernels: none -> 272 us  [the longest x2 121 us: gather(): pl.pallas_call(functools.partial(gather_kernel, levels, chunks), out_shap...]
    all_gather x2 -> x0, waiting for transfers between devices: 131 us -> none  [the longest x1 81.9 us: on_device(): everyone = lax.all_gather(grouped, 'seq', axis=1, tiled=True)]
    pmax x1 -> x0, waiting for transfers between devices: 99.8 us -> none  [on_device(): highest = lax.pmax(row_top, 'seq')]
    dot_general x7 -> x0, matrix products: 96.6 us -> none  [the longest x2 37.5 us: partial_attention(): jnp.einsum('rnhge,rphe->rnhgp', queries, keys, preferred_element_type=jnp...]
    all_gather x2 -> x0, blocking collectives: 79.5 us -> none  [the longest x1 41.1 us: on_device(): lax.all_gather(tree_keys, 'seq', axis=1, tiled=True)]
    reduce_sum x3 -> x0, other arithmetic: 29.9 us -> none  [the longest x2 29.8 us: partial_attention(): row_sum = jnp.sum(weights, axis=-1)]
    unnamed x21 -> x10, local copies, waits for them, and re-layouts: 18.8 us -> 3.4 us
  transfers between devices with their start and end apart: 5 -> 0, of which waited for: 5 -> 0; matrix products, arithmetic and copies ran while one was open for 13% -> 0% of each run, Pallas kernels for 0% -> 0%
where the time goes in v1:
time: 285 us; the launch traced here: 283 us
  Pallas kernels  272 us (95%)
  local copies, waits for them, and re-layouts  5.57 us (2%)
    pallas_call x2, Pallas kernels, gather(): pl.pallas_call(functools.partial(gather_kernel, levels, chunks), out_shap...  121 us
    pallas_call x1, Pallas kernels, scatter_merge(): pl.pallas_call(functools.partial(scatter_kernel, levels, chunks), out_sha...  73.4 us
    pallas_call x1, Pallas kernels, attend(): pl.pallas_call(functools.partial(attend_kernel, scale), grid_spec=pltpu.P...  66.5 us
    pallas_call x1, Pallas kernels, project(): pl.pallas_call(project_kernel, grid=(kv,), in_specs=[pl.BlockSpec((reques...  11.5 us

profile of v1, /device:TPU:0, one launch (start us, length us, event | category | flops | bytes accessed | tf_op | source)
XLA Modules:
  0.0 282.9 jit_solution(11153288037343304567)
XLA Ops:
  0.6 0.0 copy-start.3
  0.6 0.0 copy-start.1
  0.7 0.0 copy-start.2
  0.7 0.1 pad_add_fusion.where
  0.8 1.0 convolution_minimum_fusion.4
  1.8 0.3 convolution_minimum_fusion.3
  2.1 0.3 convolution_minimum_fusion.2
  2.3 0.3 convolution_minimum_fusion.1
  2.6 0.3 convolution_minimum_fusion
  2.8 0.3 fusion.6
  3.1 1.7 pad_maximum_fusion.mine
  4.9 63.3 %shard_map.121 = bf16[4,2,2,2,2,2,2,144,128]{8,7,6,5,4,3,2,1,0:T(8,128)(2,1)} custom-call(bf16[4,2,144,128]{3,2,1,0:T(8,128)(2,1)} %pad_maximum_fusion.mine), custom_call_target="tpu_custom_call" | custom-call | tf_op jit(solution)/shard_map/pallas_call | solution.py:219
  68.2 1.3 fusion.5
  69.5 0.1 constant_dynamic-slice_fusion
  69.6 0.0 copy-done.3
  69.6 0.0 copy-done.1
  69.6 0.0 copy-done.2
  69.6 66.5 %shard_map.122 = (bf16[4,8192,128]{2,1,0:T(8,128)(2,1)}, f32[4,64,128]{2,1,0:T(8,128)S(1)}, bf16[4,640,8,128]{3,2,1,0:T(8,128)(2,1)}, bf16[4,640,8,128]{3,2,1,0:T(8,128)(2,1)}) custom-call(s32[2]{0:T(128)S(1)} %pad_add_fusion.where, s32[4]{0:T(128)S(1)} %copy-done.2, s32[4,8]{1,0:T(4,128)S(1)} %copy-done.1, s32[4]{0:T(128)S(1)} %copy-done.3, ...), custom_call_target="tpu_custom_call" | custom-call | flops 10737418240 | bytes 20971520 | tf_op jit(solution)/shard_map/pallas_call | solution.py:456
  136.1 73.4 %shard_map.123 = bf16[4,2,128,128]{3,2,1,0:T(8,128)(2,1)S(1)} custom-call(bf16[4,2,2,2,2,2,2,128,128]{8,7,6,5,4,3,2,1,0:T(8,128)(2,1)} %bitcast.37, f32[4,2,2,2,2,2,2,1,128]{8,7,6,5,4,3,2,1,0:T(1,128)S(1)} %bitcast.32), custom_call_target="tpu_custom_call" | custom-call | tf_op jit(solution)/shard_map/pallas_call | solution.py:352
  209.5 0.8 copy.14
  210.3 57.8 %shard_map.124 = bf16[4,2,2,2,2,2,2,128,128]{8,7,6,5,4,3,2,1,0:T(8,128)(2,1)} custom-call(bf16[4,2,128,128]{3,2,1,0:T(8,128)(2,1)} %bitcast.38), custom_call_target="tpu_custom_call" | custom-call | tf_op jit(solution)/shard_map/pallas_call | solution.py:219
  268.1 0.0 copy-start
  268.1 3.4 %copy-done = bf16[4,2,2,2,2,2,2,128,128]{8,7,6,5,4,3,2,1,0:T(8,128)(2,1)S(1)} copy-done((bf16[4,2,2,2,2,2,2,128,128]{8,7,6,5,4,3,2,1,0:T(8,128)(2,1)S(1)}, bf16[4,2,2,2,2,2,2,128,128]{8,7,6,5,4,3,2,1,0:T(8,128)(2,1)}, u32[]{:S(2)}) %copy-start) | copy-done | bytes 8388632
  271.4 11.5 %shard_map.125 = bf16[256,512]{1,0:T(8,128)(2,1)} custom-call(bf16[4,8,4,16,16,128]{5,4,3,2,1,0:T(8,128)(2,1)S(1)} %bitcast.29, bf16[16384,512]{1,0:T(8,128)(2,1)} %w.1), custom_call_target="tpu_custom_call" | custom-call | tf_op jit(solution)/shard_map/pallas_call | solution.py:514
  (5 shorter events, 0.1 us)
Async XLA Ops:
  0.6 69.0 %copy-start.3 = (s32[4]{0:T(128)S(1)}, s32[4]{0:T(128)}, u32[]{:S(2)}) copy-start(s32[4]{0:T(128)} %count.1) | copy-start | bytes 52
  0.6 69.0 %copy-start.1 = (s32[4,8]{1,0:T(4,128)S(1)}, s32[4,8]{1,0:T(4,128)}, u32[]{:S(2)}) copy-start(s32[4,8]{1,0:T(4,128)} %accepted.1) | copy-start | bytes 388
  0.7 69.0 %copy-start.2 = (s32[4]{0:T(128)S(1)}, s32[4]{0:T(128)}, u32[]{:S(2)}) copy-start(s32[4]{0:T(128)} %lengths.1) | copy-start | bytes 52
  268.1 3.4 %copy-start = (bf16[4,2,2,2,2,2,2,128,128]{8,7,6,5,4,3,2,1,0:T(8,128)(2,1)S(1)}, bf16[4,2,2,2,2,2,2,128,128]{8,7,6,5,4,3,2,1,0:T(8,128)(2,1)}, u32[]{:S(2)}) copy-start(bf16[4,2,2,2,2,2,2,128,128]{8,7,6,5,4,3,2,1,0:T(8,128)(2,1)} %shard_map.124) | copy-start | bytes 25165828

commit v2 on v0

--- a/solution.py
+++ b/solution.py
@@ -1,8 +1,11 @@
+import functools
 import math
 
 import jax
 import jax.numpy as jnp
 from jax import lax
+from jax.experimental import pallas as pl
+from jax.experimental.pallas import tpu as pltpu
 from jax.sharding import PartitionSpec as P
 
 NEG = -1e30
@@ -58,7 +61,7 @@
     return jnp.where(written[:, :, None, None], placed, cache_block)
 
 
-def on_device(
+def on_device_plain(
     tree_queries,
     tree_keys,
     tree_values,
@@ -135,6 +138,556 @@
     return (projected, keys_out, values_out)
 
 
+MESH = pl.DeviceIdType.MESH
+LOG2E = math.log2(math.e)
+
+
+def bit_of(me, bit):
+    return (me // (1 << bit)) % 2
+
+
+def partner_of(me, bit):
+    return me + (1 - 2 * bit_of(me, bit)) * (1 << bit)
+
+
+def greet(me, levels):
+    barrier = pltpu.get_barrier_semaphore()
+    for bit in range(levels):
+        pl.semaphore_signal(
+            barrier, inc=1, device_id={"seq": partner_of(me, bit)}, device_id_type=MESH
+        )
+    pl.semaphore_wait(barrier, levels)
+
+
+def gather_orders(levels):
+    high = list(range(levels - 1, 2, -1))
+    return (high + [1, 2, 0], high + [2, 1, 0])
+
+
+def digits_of(value, levels):
+    return tuple((value // (1 << bit)) % 2 for bit in range(levels - 1, -1, -1))
+
+
+def gather_place(own, orders, c, p, half):
+    levels = len(own)
+    done = orders[half][:p]
+    return (
+        (c,)
+        + tuple(slice(None) if bit in done else own[bit] for bit in range(levels - 1, -1, -1))
+        + (half,)
+    )
+
+
+def gather_copy(me, own, orders, mine, out, sems, c, p, half):
+    place = gather_place(own, orders, c, p, half)
+    return pltpu.make_async_remote_copy(
+        src_ref=mine.at[c, half] if p == 0 else out.at[place],
+        dst_ref=out.at[place],
+        send_sem=sems[0].at[c, p, half],
+        recv_sem=sems[1].at[c, p, half],
+        device_id={"seq": partner_of(me, orders[half][p])},
+        device_id_type=MESH,
+    )
+
+
+def wavefront(chunks, levels):
+    return [
+        (step, step - p, p)
+        for step in range(chunks + levels)
+        for p in range(levels, 0, -1)
+        if 0 <= step - p < chunks
+    ]
+
+
+def project_kernel(levels, kv, mine, weight, out, held, weights, total, own_sem, send_sem, recv_sem, weight_sem):
+    me = lax.axis_index("seq")
+    orders = gather_orders(levels)
+    own = [bit_of(me, bit) for bit in range(levels)]
+    chunks, _, half_rows, width = mine.shape
+    depth = weight.shape[0] // kv
+    loads = [
+        pltpu.make_async_copy(
+            weight.at[pl.ds(h * depth, depth)], weights.at[pl.ds(h * depth, depth)], weight_sem.at[h]
+        )
+        for h in range(kv)
+    ]
+    greet(me, levels)
+    copy = functools.partial(gather_copy, me, own, orders, mine, held, (send_sem, recv_sem))
+    own_place = digits_of(me, levels)
+    locals_ = [
+        pltpu.make_async_copy(mine.at[c], held.at[(c,) + own_place], own_sem.at[c])
+        for c in range(chunks)
+    ]
+    for c in range(chunks):
+        for half in range(2):
+            copy(c, 0, half).start()
+    for one in locals_ + loads:
+        one.start()
+
+    kv_levels = kv.bit_length() - 1
+    parts = 1 << (levels - kv_levels)
+    group = depth // width
+    some = 2 * half_rows // group
+
+    def multiply(first, last):
+        rows = (last - first) * parts * some
+        at = first * parts * some
+
+        def body(h, carry):
+            term = None
+            for g in range(0, group, 2):
+                sides = []
+                for i in (g, g + 1):
+                    half, start = divmod(i * some, half_rows)
+                    pieces = [
+                        held[(c,) + digits_of(h, kv_levels) + digits_of(part, levels - kv_levels) + (half, pl.ds(start, some))]
+                        for c in range(first, last)
+                        for part in range(parts)
+                    ]
+                    sides.append(jnp.concatenate(pieces, axis=0))
+                left = jnp.concatenate(sides, axis=1)
+                right = weights[pl.ds(pl.multiple_of(h * depth + g * width, width), 2 * width), :]
+                now = jnp.dot(left, right, preferred_element_type=jnp.float32)
+                term = now if term is None else term + now
+            total[at : at + rows, :] += term
+            return carry
+
+        total[at : at + rows, :] = jnp.zeros((rows, total.shape[1]), jnp.float32)
+        lax.fori_loop(0, kv, body, 0)
+        out[at : at + rows, :] = total[at : at + rows, :].astype(out.dtype)
+
+    for _, c, p in wavefront(chunks, levels):
+        if p == 1:
+            locals_[c].wait()
+        for half in range(2):
+            copy(c, p - 1, half).wait_recv()
+            if p < levels:
+                copy(c, p, half).start()
+        if p == levels - 1 and c == chunks - 1:
+            for one in loads:
+                one.wait()
+            multiply(0, chunks - 1)
+    multiply(chunks - 1, chunks)
+    for c in range(chunks):
+        for p in range(levels):
+            for half in range(2):
+                copy(c, p, half).wait_send()
+
+
+def gather_project(block, weight, count, kv, collective_id):
+    chunks, _, half_rows, width = block.shape
+    levels = count.bit_length() - 1
+    columns = weight.shape[1]
+    rows = chunks * count * 2 * half_rows * width // weight.shape[0]
+    return pl.pallas_call(
+        functools.partial(project_kernel, levels, kv),
+        out_shape=jax.ShapeDtypeStruct((rows, columns), jnp.bfloat16),
+        in_specs=[pl.BlockSpec(memory_space=pl.ANY)] * 2,
+        out_specs=pl.BlockSpec(memory_space=pltpu.VMEM),
+        scratch_shapes=[
+            pltpu.VMEM((chunks,) + (2,) * levels + block.shape[1:], block.dtype),
+            pltpu.VMEM(weight.shape, weight.dtype),
+            pltpu.VMEM((rows, columns), jnp.float32),
+            pltpu.SemaphoreType.DMA((chunks,)),
+            pltpu.SemaphoreType.DMA((chunks, levels, 2)),
+            pltpu.SemaphoreType.DMA((chunks, levels, 2)),
+            pltpu.SemaphoreType.DMA((kv,)),
+        ],
+        compiler_params=pltpu.CompilerParams(
+            collective_id=collective_id, has_side_effects=True, vmem_limit_bytes=40 * 2**20
+        ),
+    )(block, weight)
+
+
+def attend_kernel(
+    scale, levels,
+    lengths, mine, k, v, own_bias, out, tree,
+    everyone, k_held, v_held, k_wide, v_wide, tree_wide,
+    work, work_s, keep, own_sem, send_sem, recv_sem, cache_sem, tree_sem, out_send, out_recv,
+    *held_all,
+):
+    me = lax.axis_index("seq")
+    orders = gather_orders(levels)
+    backward = tuple(order[::-1] for order in orders)
+    own = [bit_of(me, bit) for bit in range(levels)]
+    held, held_s = held_all[:levels], held_all[levels:]
+    requests, ctx, kv, width = k.shape
+    group = (mine.shape[2] - 2 * kv) // kv
+    heads = group * kv
+    count = 1 << levels
+    nodes = 2 * count
+    parts = count // kv
+    tile = 2 * width
+    offset = me * ctx
+
+    copy = functools.partial(gather_copy, me, own, orders, mine, everyone, (send_sem, recv_sem))
+    own_place = digits_of(me, levels)
+    loads = [
+        [
+            pltpu.make_async_copy(source.at[r], target.at[r], cache_sem.at[kind, r])
+            for kind, (source, target) in enumerate(((k, k_held), (v, v_held)))
+        ]
+        for r in range(requests)
+    ]
+
+    def own_copy(c):
+        return pltpu.make_async_copy(mine.at[c], everyone.at[(c,) + own_place], own_sem.at[c])
+
+    def tree_copy(c):
+        spread = (slice(None),) * (levels + 1)
+        return pltpu.make_async_copy(
+            everyone.at[(c,) + spread + (pl.ds(heads, 2 * kv),)], tree.at[c], tree_sem.at[c]
+        )
+
+    greet(me, levels)
+    for c in range(requests):
+        for half in range(2):
+            copy(c, 0, half).start()
+    for c in range(requests):
+        own_copy(c).start()
+    for r in range(requests):
+        for one in loads[r]:
+            one.start()
+
+    def forward(c, p):
+        if p == 1:
+            own_copy(c).wait()
+        for half in range(2):
+            copy(c, p - 1, half).wait_recv()
+            if p < levels:
+                copy(c, p, half).start()
+        if p == levels:
+            tree_copy(c).start()
+
+    diagonal = lax.broadcasted_iota(jnp.int32, (width, width), 0) == lax.broadcasted_iota(
+        jnp.int32, (width, width), 1
+    )
+
+    def block(rows, key, value, bias):
+        scores = lax.dot_general(
+            rows, key, (((1,), (1,)), ((), ())), preferred_element_type=jnp.float32
+        )
+        scores = scores * (scale * LOG2E) + bias
+        top = jnp.max(scores, axis=1, keepdims=True)
+        weights = jnp.exp2(scores - top)
+        total = jnp.sum(weights, axis=1, keepdims=True)
+        number = jnp.dot(weights.astype(jnp.bfloat16), value, preferred_element_type=jnp.float32)
+        return top, total, number
+
+    def attention(r, h):
+        @pl.when(h == 0)
+        def _():
+            for kind, (cache, rows, wide) in enumerate(((k, k_held, k_wide), (v, v_held, v_wide))):
+                pltpu.make_async_copy(cache.at[r], rows.at[r], cache_sem.at[kind, r]).wait()
+                wide[...] = rows[r].astype(jnp.float32).reshape(ctx * kv, width)
+
+        keys = k_wide[pl.ds(h, ctx, stride=kv), :].astype(jnp.bfloat16)
+        values = v_wide[pl.ds(h, ctx, stride=kv), :].astype(jnp.bfloat16)
+        position = offset + lax.broadcasted_iota(jnp.int32, (1, ctx), 1)
+        bias = jnp.where(position < lengths[r], 0.0, NEG)
+        everything = (slice(None),) * (levels + 1)
+
+        def queries(part):
+            low = levels - (parts.bit_length() - 1)
+            where = digits_of(part, levels - low) + (slice(None),) * (low + 1)
+            found = everyone[(r,) + where + (pl.ds(pl.multiple_of(h * group, group), group),)]
+            return found.reshape(tile, width)
+
+        def store(part, top, total, number):
+            number = (number * (1.0 / total)).astype(jnp.bfloat16)
+            lines = top + jnp.log2(total)
+            place = (r,) + digits_of(h * parts + part, levels)
+            for half in range(2):
+                span = slice(half * width, (half + 1) * width)
+                work[place + (half,)] = number[span]
+                work_s[place + (half,)] = jnp.sum(
+                    jnp.where(diagonal, lines[span], 0.0), axis=0, keepdims=True
+                )
+
+        for part in range(parts):
+            store(part, *block(queries(part), keys, values, bias))
+
+        @pl.when(r * kv + h == me)
+        def _():
+            tree_wide[...] = (
+                everyone[(r,) + everything + (pl.ds(heads, 2 * kv),)]
+                .astype(jnp.float32)
+                .reshape(nodes * 2 * kv, width)
+            )
+            own_k = tree_wide[pl.ds(h, nodes, stride=2 * kv), :].astype(jnp.bfloat16)
+            own_v = tree_wide[pl.ds(kv + h, nodes, stride=2 * kv), :].astype(jnp.bfloat16)
+            for part in range(parts):
+                rows = queries(part)
+                top, total, number = block(rows, keys, values, bias)
+                t_top, t_total, t_number = block(
+                    rows, own_k, own_v, own_bias[part * tile : (part + 1) * tile]
+                )
+                high = jnp.maximum(top, t_top)
+                fa, fb = jnp.exp2(top - high), jnp.exp2(t_top - high)
+                store(part, high, total * fa + t_total * fb, number * fa + t_number * fb)
+
+    def send(c, p, half):
+        bit_now = backward[half][p]
+        done = backward[half][:p]
+        where = tuple(
+            own[bit] if bit in done else 1 - own[bit] if bit == bit_now else slice(None)
+            for bit in range(levels - 1, -1, -1)
+        )
+        place = (c,) + where + (half,)
+        return [
+            pltpu.make_async_remote_copy(
+                src_ref=source.at[place],
+                dst_ref=target.at[c, half],
+                send_sem=out_send.at[kind, c, p, half],
+                recv_sem=out_recv.at[kind, c, p, half],
+                device_id={"seq": partner_of(me, bit_now)},
+                device_id_type=MESH,
+            )
+            for kind, (source, target) in enumerate(((work, held[p]), (work_s, held_s[p])))
+        ]
+
+    def merge(c, p, half):
+        order = backward[half]
+        done = order[: p + 1]
+        last = p == levels - 1
+
+        def one(k, kept):
+            fixed = {bit: own[bit] for bit in done}
+            if not last:
+                fixed[order[p + 1]] = own[order[p + 1]] if kept else 1 - own[order[p + 1]]
+            free = [bit for bit in range(levels - 1, -1, -1) if bit not in fixed]
+            for rank, bit in enumerate(reversed(free)):
+                fixed[bit] = (k // (1 << rank)) % 2
+            at_work = (c,) + tuple(fixed[bit] for bit in range(levels - 1, -1, -1)) + (half,)
+            at_held = (c, half) + tuple(
+                fixed[bit] for bit in range(levels - 1, -1, -1) if bit not in done
+            )
+            at_keep = (c, half) + tuple(
+                fixed[bit] for bit in range(levels - 1, -1, -1) if bit not in order[:2]
+            )
+            log_a, log_b = work_s[at_work], held_s[p][at_held]
+            top = jnp.maximum(log_a, log_b)
+            part_a, part_b = jnp.exp2(log_a - top), jnp.exp2(log_b - top)
+            total = part_a + part_b
+            share = jnp.sum(jnp.where(diagonal, part_a / total, 0.0), axis=1, keepdims=True)
+            here = work[at_work].astype(jnp.float32) if p == 0 else keep[at_keep]
+            merged = here * share + held[p][at_held].astype(jnp.float32) * (1.0 - share)
+            if last:
+                out[c, half] = merged.astype(jnp.bfloat16)
+                return
+            if kept:
+                keep[at_keep] = merged
+            else:
+                work[at_work] = merged.astype(jnp.bfloat16)
+            work_s[at_work] = top + jnp.log2(total)
+
+        if last:
+            one(0, True)
+            return
+        for kept in (False, True):
+            size = 1 << (levels - 2 - p)
+            if size == 1:
+                one(0, kept)
+            else:
+                lax.fori_loop(0, size, lambda k, carry, kept=kept: (one(k, kept), carry)[1], 0)
+            if not kept:
+                for pending in send(c, p + 1, half):
+                    pending.start()
+
+    def reduce(c, p):
+        for half in range(2):
+            if p == 0:
+                for one in send(c, 0, half):
+                    one.start()
+            else:
+                for one in send(c, p - 1, half):
+                    one.wait_recv()
+                merge(c, p - 1, half)
+
+    events = []
+    late = {}
+    for step, c, p in wavefront(requests, levels):
+        if step <= levels:
+            forward(c, p)
+        else:
+            late.setdefault(step, []).append((c, p))
+    for step, found in late.items():
+        after = step - levels
+        for c, p in found:
+            if p == levels:
+                slot = c * kv - 1
+            else:
+                slot = min((after - 1) * kv + (3 if p == levels - 1 else 1), c * kv - 2)
+            events.append((slot, 0, -c, functools.partial(forward, c, p)))
+    for c in range(requests):
+        base = (c + 1) * kv - 1
+        for p, wait in enumerate((0, 2, 5, 8, 10, 12)[: levels + 1]):
+            events.append((base + wait, 1, -c, functools.partial(reduce, c, p)))
+    events.sort(key=lambda e: e[:3])
+    total_steps = requests * kv
+
+    def step_body(i, carry):
+        attention(i // kv, i % kv)
+        for slot, _, _, act in events:
+            if slot < total_steps:
+                pl.when(i == slot)(act)
+        return carry
+
+    lax.fori_loop(0, total_steps, step_body, 0)
+    for slot, _, _, act in events:
+        if slot >= total_steps:
+            act()
+    for c in range(requests):
+        tree_copy(c).wait()
+        for p in range(levels):
+            for half in range(2):
+                copy(c, p, half).wait_send()
+                for one in send(c, p, half):
+                    one.wait_send()
+
+
+def attend(scale, count, lengths, mine, k, v, own_bias, collective_id):
+    requests, ctx, kv, width = k.shape
+    levels = count.bit_length() - 1
+    bits = (2,) * levels
+    rows = 2 * mine.shape[2] - 4 * kv
+    half_rows = rows // 2
+    work = requests * kv * own_bias.shape[0] * ctx
+    hbm = pl.BlockSpec(memory_space=pl.ANY)
+    vmem = pl.BlockSpec(memory_space=pltpu.VMEM)
+    held = [
+        pltpu.VMEM((requests, 2) + bits[: levels - 1 - p] + (half_rows, width), jnp.bfloat16)
+        for p in range(levels)
+    ]
+    held_s = [
+        pltpu.VMEM((requests, 2) + bits[: levels - 1 - p] + (1, half_rows), jnp.float32)
+        for p in range(levels)
+    ]
+    return pl.pallas_call(
+        functools.partial(attend_kernel, scale, levels),
+        in_specs=[pl.BlockSpec(memory_space=pltpu.SMEM), hbm, hbm, hbm, vmem],
+        out_specs=[vmem, hbm],
+        out_shape=[
+            jax.ShapeDtypeStruct((requests, 2, half_rows, width), jnp.bfloat16),
+            jax.ShapeDtypeStruct((requests,) + bits + (2, 2 * kv, width), mine.dtype),
+        ],
+        scratch_shapes=[
+            pltpu.VMEM((requests,) + bits + mine.shape[1:], mine.dtype),
+            pltpu.VMEM(k.shape, k.dtype),
+            pltpu.VMEM(v.shape, v.dtype),
+            pltpu.VMEM((ctx * kv, width), jnp.float32),
+            pltpu.VMEM((ctx * kv, width), jnp.float32),
+            pltpu.VMEM((2 * count * 2 * kv, width), jnp.float32),
+            pltpu.VMEM((requests,) + bits + (2, half_rows, width), jnp.bfloat16),
+            pltpu.VMEM((requests,) + bits + (2, 1, half_rows), jnp.float32),
+            pltpu.VMEM((requests, 2) + bits[2:] + (half_rows, width), jnp.float32),
+            pltpu.SemaphoreType.DMA((requests,)),
+            pltpu.SemaphoreType.DMA((requests, levels, 2)),
+            pltpu.SemaphoreType.DMA((requests, levels, 2)),
+            pltpu.SemaphoreType.DMA((2, requests)),
+            pltpu.SemaphoreType.DMA((requests,)),
+            pltpu.SemaphoreType.DMA((2, requests, levels, 2)),
+            pltpu.SemaphoreType.DMA((2, requests, levels, 2)),
+        ]
+        + held
+        + held_s,
+        compiler_params=pltpu.CompilerParams(
+            collective_id=collective_id, has_side_effects=True, vmem_limit_bytes=60 * 2**20
+        ),
+        cost_estimate=pl.CostEstimate(
+            flops=4 * work * width, bytes_accessed=4 * k.size * 2, transcendentals=work
+        ),
+    )(lengths, mine, k, v, own_bias)
+
+
+def append_kernel(where, lengths, accepted, count, k, v, tree, k_out, v_out):
+    r = pl.program_id(0)
+    ctx, kv = k.shape[1:3]
+    for kind, (cache, target) in enumerate(((k, k_out), (v, v_out))):
+        target[...] = cache[...]
+        for j in range(accepted.shape[1]):
+            slot = lengths[r] + j - where[0]
+
+            @pl.when((j < count[r]) & (slot >= 0) & (slot < ctx))
+            def _():
+                target[0, slot] = tree[0, accepted[r, j], kind]
+
+
+def append(where, lengths, accepted, count, k, v, tree):
+    requests, ctx, kv, width = k.shape
+    cache = pl.BlockSpec((1, ctx, kv, width), lambda r, *_: (r, 0, 0, 0))
+    return pl.pallas_call(
+        append_kernel,
+        grid_spec=pltpu.PrefetchScalarGridSpec(
+            num_scalar_prefetch=4,
+            grid=(requests,),
+            in_specs=[
+                cache, cache,
+                pl.BlockSpec((1,) + tree.shape[1:], lambda r, *_: (r, 0, 0, 0, 0)),
+            ],
+            out_specs=[cache, cache],
+        ),
+        out_shape=[jax.ShapeDtypeStruct(k.shape, k.dtype)] * 2,
+        compiler_params=pltpu.CompilerParams(vmem_limit_bytes=24 * 2**20),
+    )(where, lengths, accepted, count, k, v, tree)
+
+
+def on_device(
+    tree_queries,
+    tree_keys,
+    tree_values,
+    cache_keys,
+    cache_values,
+    out_weight,
+    context_lengths,
+    parents,
+    accepted_nodes,
+    accepted_count,
+):
+    requests, ctx, kv, width = cache_keys.shape
+    node_local, heads = tree_queries.shape[1:3]
+    group = heads // kv
+    count = lax.axis_size("seq")
+    nodes = node_local * count
+    part = kv * nodes // count
+    me = lax.axis_index("seq")
+    sent = jnp.concatenate([tree_queries, tree_keys, tree_values], axis=2)
+    own_request = lax.rem(me, requests * kv) // kv
+    own_reach = lax.dynamic_index_in_dim(ancestors(parents), own_request, 0, keepdims=False)
+    own_bias = jnp.repeat(jnp.where(own_reach > 0.5, 0.0, NEG), group, axis=0)
+    home, tree = attend(
+        1.0 / math.sqrt(width), count, context_lengths, sent, cache_keys, cache_values, own_bias, 1
+    )
+    home = home.reshape(requests, part, group, width).swapaxes(1, 2)
+    projected = gather_project(
+        home.reshape(requests, 2, part * group // 2, width), out_weight, count, kv, 2
+    )
+    keys_out, values_out = append(
+        (me * ctx).astype(jnp.int32).reshape(1),
+        context_lengths, accepted_nodes, accepted_count, cache_keys, cache_values,
+        tree.reshape(requests, nodes, 2, kv, width),
+    )
+    return (projected, keys_out, values_out)
+
+
+def fits(mesh, args):
+    queries, keys = args[0], args[3]
+    count, split = mesh.shape["seq"], mesh.shape["head"]
+    requests, nodes, heads, width = queries.shape
+    kv = keys.shape[2]
+    rows = nodes * heads // count
+    return (
+        split == 1
+        and count >= 8
+        and count & (count - 1) == 0
+        and count % kv == 0
+        and count >= requests * kv
+        and nodes * kv // count % 16 == 0
+        and nodes == 2 * count
+        and rows == 2 * width
+    )
+
+
 def solution(mesh):
     in_specs = (
         P(None, "seq", "head", None),
@@ -149,6 +702,11 @@
         P(),
     )
     out_specs = (P("head", "seq"), P(None, "seq", "head", None), P(None, "seq", "head", None))
-    return jax.shard_map(
-        on_device, mesh=mesh, in_specs=in_specs, out_specs=out_specs, check_vma=False
-    )
+
+    def run(*args):
+        body = on_device if fits(mesh, args) else on_device_plain
+        return jax.shard_map(
+            body, mesh=mesh, in_specs=in_specs, out_specs=out_specs, check_vma=False
+        )(*args)
+
+    return run

time: 780 us -> 252 us (0.32)
  waiting for transfers between devices: 520 us -> 0 us
  Pallas kernels: 0 us -> 237 us
  matrix products: 98.1 us -> 2.29 us
  blocking collectives: 79.5 us -> 0 us
  other arithmetic: 33 us -> 1.75 us
  local copies, waits for them, and re-layouts: 34.4 us -> 7.54 us
  between operations: 14 us -> 0.81 us
    unnamed x6 -> x0, waiting for transfers between devices: 280 us -> none
    pallas_call x0 -> x3, Pallas kernels: none -> 237 us  [the longest x1 173 us: attend(): pl.pallas_call(functools.partial(attend_kernel, scale, levels), in_specs=...]
    all_gather x2 -> x0, waiting for transfers between devices: 131 us -> none  [the longest x1 81.9 us: on_device(): everyone = lax.all_gather(grouped, 'seq', axis=1, tiled=True)]
    pmax x1 -> x0, waiting for transfers between devices: 99.8 us -> none  [on_device(): highest = lax.pmax(row_top, 'seq')]
    dot_general x7 -> x0, matrix products: 96.6 us -> none  [the longest x2 37.5 us: partial_attention(): jnp.einsum('rnhge,rphe->rnhgp', queries, keys, preferred_element_type=jnp...]
    all_gather x2 -> x0, blocking collectives: 79.5 us -> none  [the longest x1 41.1 us: on_device(): lax.all_gather(tree_keys, 'seq', axis=1, tiled=True)]
    reduce_sum x3 -> x0, other arithmetic: 29.9 us -> none  [the longest x2 29.8 us: partial_attention(): row_sum = jnp.sum(weights, axis=-1)]
    unnamed x21 -> x13, local copies, waits for them, and re-layouts: 18.8 us -> 5.69 us
  transfers between devices with their start and end apart: 5 -> 0, of which waited for: 5 -> 0; matrix products, arithmetic and copies ran while one was open for 13% -> 0% of each run, Pallas kernels for 0% -> 0%
where the time goes in v2:
time: 252 us; the launch traced here: 250 us
  Pallas kernels  237 us (94%)
  local copies, waits for them, and re-layouts  7.54 us (3%)
    pallas_call x1, Pallas kernels, attend(): pl.pallas_call(functools.partial(attend_kernel, scale, levels), in_specs=...  173 us
    pallas_call x1, Pallas kernels, gather_project(): pl.pallas_call(functools.partial(project_kernel, levels, kv), out_shape=j...  59.2 us
    unnamed x13, local copies, waits for them, and re-layouts  5.69 us
    pallas_call x1, Pallas kernels, append(): pl.pallas_call(append_kernel, grid_spec=pltpu.PrefetchScalarGridSpec(num_...  5.07 us

profile of v2, /device:TPU:0, one launch (start us, length us, event | category | flops | bytes accessed | tf_op | source)
XLA Modules:
  0.0 249.6 jit_solution(17199314847975110711)
XLA Ops:
  0.7 1.0 convolution_minimum_fusion.4
  1.7 0.3 convolution_minimum_fusion.3
  2.0 0.3 convolution_minimum_fusion.2
  2.2 0.3 convolution_minimum_fusion.1
  2.5 0.3 convolution_minimum_fusion
  2.7 0.3 fusion.5
  3.0 1.7 pad_maximum_fusion.mine
  4.8 0.8 broadcast_in_dim.18
  5.6 172.9 %shard_map.121 = (bf16[4,2,128,128]{3,2,1,0:T(8,128)(2,1)}, bf16[4,2,2,2,2,2,2,16,128]{8,7,6,5,4,3,2,1,0:T(8,128)(2,1)}) custom-call(s32[4]{0:T(128)} %lengths.3, bf16[4,2,144,128]{3,2,1,0:T(8,128)(2,1)} %pad_maximum_fusion.mine, bf16[4,640,8,128]{3,2,1,0:T(8,128)(2,1)} %k.3, bf16[4,640,8,128]{3,2,1,0:T(8,128)(2,1)} %v.3, f32[1024,64]{1,0:T(8,128)} %bitcast.21), custom_call_target="tpu_custom_call" | custom-call | flops 10737418240 | bytes 20971520 | tf_op jit(solution)/shard_map/pallas_call | solution.py:566
  178.5 1.0 copy.13
  179.5 0.0 copy-start.2
  179.6 0.0 copy-start.3
  179.6 0.0 copy-start.4
  179.6 0.0 copy-start.5
  179.6 59.2 %shard_map.122 = bf16[256,512]{1,0:T(8,128)(2,1)S(1)} custom-call(bf16[4,2,128,128]{3,2,1,0:T(8,128)(2,1)S(1)} %bitcast.19, bf16[16384,512]{1,0:T(8,128)(2,1)} %weight.1), custom_call_target="tpu_custom_call" | custom-call | tf_op jit(solution)/shard_map/pallas_call | solution.py:282
  238.8 0.0 copy-done.2
  238.8 0.0 copy-done.3
  238.8 0.0 copy-done.4
  238.8 0.0 copy-done.5
  238.9 0.0 copy-start
  238.9 2.5 copy-done
  241.3 0.0 copy-start.1
  241.3 2.5 copy-done.1
  243.8 5.1 %shard_map.123 = (bf16[4,640,8,128]{3,2,1,0:T(8,128)(2,1)}, bf16[4,640,8,128]{3,2,1,0:T(8,128)(2,1)}) custom-call(s32[1]{0:T(128)} %bitcast.5.where, s32[4]{0:T(128)S(1)} %copy-done.4, s32[4,8]{1,0:T(4,128)S(1)} %copy-done.3, s32[4]{0:T(128)S(1)} %copy-done.5, bf16[4,640,8,128]{3,2,1,0:T(8,128)(2,1)S(1)} %copy-done, bf16[4,640,8,128]{3,2,1,0:T(8,128)(2,1)S(1)} %copy-done.1, ...), custom_call_target="tpu_custom_call" | custom-call | tf_op jit(solution)/shard_map/pallas_call | solution.py:619
  248.9 0.7 copy.15
  (2 shorter events, 0.0 us)
Async XLA Ops:
  179.5 59.3 %copy-start.2 = (bf16[4,2,2,2,2,2,2,16,128]{8,7,6,5,4,3,2,1,0:T(8,128)(2,1)S(1)}, bf16[4,2,2,2,2,2,2,16,128]{8,7,6,5,4,3,2,1,0:T(8,128)(2,1)}, u32[]{:S(2)}) copy-start(bf16[4,2,2,2,2,2,2,16,128]{8,7,6,5,4,3,2,1,0:T(8,128)(2,1)} %get-tuple-element.8) | copy-start | bytes 3145732
  179.6 59.3 %copy-start.3 = (s32[4,8]{1,0:T(4,128)S(1)}, s32[4,8]{1,0:T(4,128)}, u32[]{:S(2)}) copy-start(s32[4,8]{1,0:T(4,128)} %accepted.1) | copy-start | bytes 388
  179.6 59.3 %copy-start.4 = (s32[4]{0:T(128)S(1)}, s32[4]{0:T(128)}, u32[]{:S(2)}) copy-start(s32[4]{0:T(128)} %lengths.3) | copy-start | bytes 52
  179.6 59.3 %copy-start.5 = (s32[4]{0:T(128)S(1)}, s32[4]{0:T(128)}, u32[]{:S(2)}) copy-start(s32[4]{0:T(128)} %count.1) | copy-start | bytes 52
  238.9 2.5 copy-start
  241.3 2.5 copy-start.1

commit v3 on v2

--- a/solution.py
+++ b/solution.py
@@ -199,7 +199,7 @@
     ]
 
 
-def project_kernel(levels, kv, mine, weight, out, held, weights, total, own_sem, send_sem, recv_sem, weight_sem):
+def project_kernel(levels, kv, cuts, mine, weight, out, held, weights, total, own_sem, send_sem, recv_sem, weight_sem):
     me = lax.axis_index("seq")
     orders = gather_orders(levels)
     own = [bit_of(me, bit) for bit in range(levels)]
@@ -218,16 +218,22 @@
         pltpu.make_async_copy(mine.at[c], held.at[(c,) + own_place], own_sem.at[c])
         for c in range(chunks)
     ]
-    for c in range(chunks):
-        for half in range(2):
-            copy(c, 0, half).start()
+
+    def begin(c):
+        if c < chunks:
+            for half in range(2):
+                copy(c, 0, half).start()
+
+    begin(0)
+    begin(1)
     for one in locals_ + loads:
         one.start()
 
     kv_levels = kv.bit_length() - 1
     parts = 1 << (levels - kv_levels)
     group = depth // width
-    some = 2 * half_rows // group
+    requests = chunks // cuts
+    some = cuts * 2 * half_rows // group
 
     def multiply(first, last):
         rows = (last - first) * parts * some
@@ -238,10 +244,11 @@
             for g in range(0, group, 2):
                 sides = []
                 for i in (g, g + 1):
-                    half, start = divmod(i * some, half_rows)
+                    cut, start = divmod(i * some, 2 * half_rows)
+                    half, start = divmod(start, half_rows)
                     pieces = [
-                        held[(c,) + digits_of(h, kv_levels) + digits_of(part, levels - kv_levels) + (half, pl.ds(start, some))]
-                        for c in range(first, last)
+                        held[(r * cuts + cut,) + digits_of(h, kv_levels) + digits_of(part, levels - kv_levels) + (half, pl.ds(start, some))]
+                        for r in range(first, last)
                         for part in range(parts)
                     ]
                     sides.append(jnp.concatenate(pieces, axis=0))
@@ -263,24 +270,26 @@
             copy(c, p - 1, half).wait_recv()
             if p < levels:
                 copy(c, p, half).start()
+        if p == 1:
+            begin(c + 2)
         if p == levels - 1 and c == chunks - 1:
             for one in loads:
                 one.wait()
-            multiply(0, chunks - 1)
-    multiply(chunks - 1, chunks)
+            multiply(0, requests - 1)
+    multiply(requests - 1, requests)
     for c in range(chunks):
         for p in range(levels):
             for half in range(2):
                 copy(c, p, half).wait_send()
 
 
-def gather_project(block, weight, count, kv, collective_id):
+def gather_project(block, weight, count, kv, cuts, collective_id):
     chunks, _, half_rows, width = block.shape
     levels = count.bit_length() - 1
     columns = weight.shape[1]
     rows = chunks * count * 2 * half_rows * width // weight.shape[0]
     return pl.pallas_call(
-        functools.partial(project_kernel, levels, kv),
+        functools.partial(project_kernel, levels, kv, cuts),
         out_shape=jax.ShapeDtypeStruct((rows, columns), jnp.bfloat16),
         in_specs=[pl.BlockSpec(memory_space=pl.ANY)] * 2,
         out_specs=pl.BlockSpec(memory_space=pltpu.VMEM),
@@ -340,9 +349,14 @@
         )
 
     greet(me, levels)
-    for c in range(requests):
-        for half in range(2):
-            copy(c, 0, half).start()
+
+    def begin(c):
+        if c < requests:
+            for half in range(2):
+                copy(c, 0, half).start()
+
+    begin(0)
+    begin(1)
     for c in range(requests):
         own_copy(c).start()
     for r in range(requests):
@@ -363,10 +377,12 @@
         jnp.int32, (width, width), 1
     )
 
-    def block(rows, key, value, bias):
-        scores = lax.dot_general(
+    def score(rows, key):
+        return lax.dot_general(
             rows, key, (((1,), (1,)), ((), ())), preferred_element_type=jnp.float32
         )
+
+    def block(scores, value, bias):
         scores = scores * (scale * LOG2E) + bias
         top = jnp.max(scores, axis=1, keepdims=True)
         weights = jnp.exp2(scores - top)
@@ -404,8 +420,12 @@
                     jnp.where(diagonal, lines[span], 0.0), axis=0, keepdims=True
                 )
 
+        ahead = score(queries(0), keys)
         for part in range(parts):
-            store(part, *block(queries(part), keys, values, bias))
+            scores = ahead
+            if part + 1 < parts:
+                ahead = score(queries(part + 1), keys)
+            store(part, *block(scores, values, bias))
 
         @pl.when(r * kv + h == me)
         def _():
@@ -418,9 +438,9 @@
             own_v = tree_wide[pl.ds(kv + h, nodes, stride=2 * kv), :].astype(jnp.bfloat16)
             for part in range(parts):
                 rows = queries(part)
-                top, total, number = block(rows, keys, values, bias)
+                top, total, number = block(score(rows, keys), values, bias)
                 t_top, t_total, t_number = block(
-                    rows, own_k, own_v, own_bias[part * tile : (part + 1) * tile]
+                    score(rows, own_k), own_v, own_bias[part * tile : (part + 1) * tile]
                 )
                 high = jnp.maximum(top, t_top)
                 fa, fb = jnp.exp2(top - high), jnp.exp2(t_top - high)
@@ -509,6 +529,8 @@
     for step, c, p in wavefront(requests, levels):
         if step <= levels:
             forward(c, p)
+            if p == 1:
+                begin(step + 1)
         else:
             late.setdefault(step, []).append((c, p))
     for step, found in late.items():
@@ -521,7 +543,7 @@
             events.append((slot, 0, -c, functools.partial(forward, c, p)))
     for c in range(requests):
         base = (c + 1) * kv - 1
-        for p, wait in enumerate((0, 2, 5, 8, 10, 12)[: levels + 1]):
+        for p, wait in enumerate((0, 2, 7, 11, 13, 15)[: levels + 1]):
             events.append((base + wait, 1, -c, functools.partial(reduce, c, p)))
     events.sort(key=lambda e: e[:3])
     total_steps = requests * kv
@@ -628,7 +650,7 @@
             out_specs=[cache, cache],
         ),
         out_shape=[jax.ShapeDtypeStruct(k.shape, k.dtype)] * 2,
-        compiler_params=pltpu.CompilerParams(vmem_limit_bytes=24 * 2**20),
+        compiler_params=pltpu.CompilerParams(vmem_limit_bytes=60 * 2**20),
     )(where, lengths, accepted, count, k, v, tree)
 
 
@@ -659,8 +681,10 @@
         1.0 / math.sqrt(width), count, context_lengths, sent, cache_keys, cache_values, own_bias, 1
     )
     home = home.reshape(requests, part, group, width).swapaxes(1, 2)
+    cuts = 2
     projected = gather_project(
-        home.reshape(requests, 2, part * group // 2, width), out_weight, count, kv, 2
+        home.reshape(requests * cuts, 2, part * group // (2 * cuts), width),
+        out_weight, count, kv, cuts, 2,
     )
     keys_out, values_out = append(
         (me * ctx).astype(jnp.int32).reshape(1),

time: 252 us -> 245 us (0.972)
  local copies, waits for them, and re-layouts: 7.54 us -> 2.55 us
    pallas_call x1, Pallas kernels: 173 us -> 156 us  [attend(): pl.pallas_call(functools.partial(attend_kernel, scale, levels), in_specs=...]
    pallas_call x1, Pallas kernels: 59.2 us -> 72.1 us  [gather_project(): pl.pallas_call(functools.partial(project_kernel, levels, kv, cuts), out_s...]
    unnamed x13 -> x1, local copies, waits for them, and re-layouts: 5.69 us -> 0.7 us
    pallas_call x1, Pallas kernels: 5.07 us -> 9.25 us  [append(): pl.pallas_call(append_kernel, grid_spec=pltpu.PrefetchScalarGridSpec(num_...]
where the time goes in v3:
time: 245 us; the launch traced here: 244 us
  Pallas kernels  237 us (97%)
  local copies, waits for them, and re-layouts  2.55 us (1%)
    pallas_call x1, Pallas kernels, attend(): pl.pallas_call(functools.partial(attend_kernel, scale, levels), in_specs=...  156 us
    pallas_call x1, Pallas kernels, gather_project(): pl.pallas_call(functools.partial(project_kernel, levels, kv, cuts), out_s...  72.1 us
    pallas_call x1, Pallas kernels, append(): pl.pallas_call(append_kernel, grid_spec=pltpu.PrefetchScalarGridSpec(num_...  9.25 us

profile of v3, /device:TPU:0, one launch (start us, length us, event | category | flops | bytes accessed | tf_op | source)
XLA Modules:
  0.0 244.3 jit_solution(151995287824504742)
XLA Ops:
  0.7 1.0 convolution_minimum_fusion.4
  1.7 0.3 convolution_minimum_fusion.3
  2.0 0.3 convolution_minimum_fusion.2
  2.2 0.3 convolution_minimum_fusion.1
  2.5 0.3 convolution_minimum_fusion
  2.7 0.3 fusion.5
  3.0 1.7 pad_maximum_fusion.mine
  4.8 0.8 broadcast_in_dim.18
  5.6 155.6 %shard_map.121 = (bf16[4,2,128,128]{3,2,1,0:T(8,128)(2,1)}, bf16[4,2,2,2,2,2,2,16,128]{8,7,6,5,4,3,2,1,0:T(8,128)(2,1)}) custom-call(s32[4]{0:T(128)} %lengths.3, bf16[4,2,144,128]{3,2,1,0:T(8,128)(2,1)} %pad_maximum_fusion.mine, bf16[4,640,8,128]{3,2,1,0:T(8,128)(2,1)} %k.3, bf16[4,640,8,128]{3,2,1,0:T(8,128)(2,1)} %v.3, f32[1024,64]{1,0:T(8,128)} %bitcast.21), custom_call_target="tpu_custom_call" | custom-call | flops 10737418240 | bytes 20971520 | tf_op jit(solution)/shard_map/pallas_call | solution.py:588
  161.2 1.0 copy.13
  162.2 72.1 %shard_map.122 = bf16[256,512]{1,0:T(8,128)(2,1)S(1)} custom-call(bf16[8,2,64,128]{3,2,1,0:T(8,128)(2,1)S(1)} %bitcast.19, bf16[16384,512]{1,0:T(8,128)(2,1)} %weight.1), custom_call_target="tpu_custom_call" | custom-call | tf_op jit(solution)/shard_map/pallas_call | solution.py:291
  234.3 9.3 %shard_map.123 = (bf16[4,640,8,128]{3,2,1,0:T(8,128)(2,1)}, bf16[4,640,8,128]{3,2,1,0:T(8,128)(2,1)}) custom-call(s32[1]{0:T(128)} %bitcast.5.where, s32[4]{0:T(128)} %lengths.3, s32[4,8]{1,0:T(4,128)} %accepted.1, s32[4]{0:T(128)} %count.1, bf16[4,640,8,128]{3,2,1,0:T(8,128)(2,1)} %k.3, bf16[4,640,8,128]{3,2,1,0:T(8,128)(2,1)} %v.3, ...), custom_call_target="tpu_custom_call" | custom-call | tf_op jit(solution)/shard_map/pallas_call | solution.py:641
  243.6 0.7 copy.15
  (2 shorter events, 0.0 us)

commit v4 on v3

--- a/solution.py
+++ b/solution.py
@@ -219,13 +219,9 @@
         for c in range(chunks)
     ]
 
-    def begin(c):
-        if c < chunks:
-            for half in range(2):
-                copy(c, 0, half).start()
-
-    begin(0)
-    begin(1)
+    for c in range(chunks):
+        for half in range(2):
+            copy(c, 0, half).start()
     for one in locals_ + loads:
         one.start()
 
@@ -270,8 +266,6 @@
             copy(c, p - 1, half).wait_recv()
             if p < levels:
                 copy(c, p, half).start()
-        if p == 1:
-            begin(c + 2)
         if p == levels - 1 and c == chunks - 1:
             for one in loads:
                 one.wait()
@@ -390,13 +384,13 @@
         number = jnp.dot(weights.astype(jnp.bfloat16), value, preferred_element_type=jnp.float32)
         return top, total, number
 
+    def widen(r):
+        for kind, (cache, rows, wide) in enumerate(((k, k_held, k_wide), (v, v_held, v_wide))):
+            pltpu.make_async_copy(cache.at[r], rows.at[r], cache_sem.at[kind, r]).wait()
+            wide[...] = rows[r].astype(jnp.float32).reshape(ctx * kv, width)
+
     def attention(r, h):
-        @pl.when(h == 0)
-        def _():
-            for kind, (cache, rows, wide) in enumerate(((k, k_held, k_wide), (v, v_held, v_wide))):
-                pltpu.make_async_copy(cache.at[r], rows.at[r], cache_sem.at[kind, r]).wait()
-                wide[...] = rows[r].astype(jnp.float32).reshape(ctx * kv, width)
-
+        pl.when((h == 0) & (r > 0))(functools.partial(widen, r))
         keys = k_wide[pl.ds(h, ctx, stride=kv), :].astype(jnp.bfloat16)
         values = v_wide[pl.ds(h, ctx, stride=kv), :].astype(jnp.bfloat16)
         position = offset + lax.broadcasted_iota(jnp.int32, (1, ctx), 1)
@@ -528,6 +522,8 @@
     late = {}
     for step, c, p in wavefront(requests, levels):
         if step <= levels:
+            if (c, p) == (0, levels):
+                widen(0)
             forward(c, p)
             if p == 1:
                 begin(step + 1)
@@ -625,10 +621,11 @@
 def append_kernel(where, lengths, accepted, count, k, v, tree, k_out, v_out):
     r = pl.program_id(0)
     ctx, kv = k.shape[1:3]
+    start = where[0] + pl.program_id(1) * ctx
     for kind, (cache, target) in enumerate(((k, k_out), (v, v_out))):
         target[...] = cache[...]
         for j in range(accepted.shape[1]):
-            slot = lengths[r] + j - where[0]
+            slot = lengths[r] + j - start
 
             @pl.when((j < count[r]) & (slot >= 0) & (slot < ctx))
             def _():
@@ -637,15 +634,16 @@
 
 def append(where, lengths, accepted, count, k, v, tree):
     requests, ctx, kv, width = k.shape
-    cache = pl.BlockSpec((1, ctx, kv, width), lambda r, *_: (r, 0, 0, 0))
+    cuts = 2 if ctx % 2 == 0 else 1
+    cache = pl.BlockSpec((1, ctx // cuts, kv, width), lambda r, b, *_: (r, b, 0, 0))
     return pl.pallas_call(
         append_kernel,
         grid_spec=pltpu.PrefetchScalarGridSpec(
             num_scalar_prefetch=4,
-            grid=(requests,),
+            grid=(requests, cuts),
             in_specs=[
                 cache, cache,
-                pl.BlockSpec((1,) + tree.shape[1:], lambda r, *_: (r, 0, 0, 0, 0)),
+                pl.BlockSpec((1,) + tree.shape[1:], lambda r, b, *_: (r, 0, 0, 0, 0)),
             ],
             out_specs=[cache, cache],
         ),
@@ -681,7 +679,7 @@
         1.0 / math.sqrt(width), count, context_lengths, sent, cache_keys, cache_values, own_bias, 1
     )
     home = home.reshape(requests, part, group, width).swapaxes(1, 2)
-    cuts = 2
+    cuts = 1
     projected = gather_project(
         home.reshape(requests * cuts, 2, part * group // (2 * cuts), width),
         out_weight, count, kv, cuts, 2,

time: 245 us -> 236 us (0.963)
  Pallas kernels: 237 us -> 229 us
    pallas_call x1, Pallas kernels: 72.1 us -> 61.3 us  [gather_project(): pl.pallas_call(functools.partial(project_kernel, levels, kv, cuts), out_s...]
where the time goes in v4:
time: 236 us
  Pallas kernels  229 us (97%)
  local copies, waits for them, and re-layouts  2.55 us (1%)
    pallas_call x1, Pallas kernels, attend(): pl.pallas_call(functools.partial(attend_kernel, scale, levels), in_specs=...  156 us
    pallas_call x1, Pallas kernels, gather_project(): pl.pallas_call(functools.partial(project_kernel, levels, kv, cuts), out_s...  61.3 us
    pallas_call x1, Pallas kernels, append(): pl.pallas_call(append_kernel, grid_spec=pltpu.PrefetchScalarGridSpec(num_...  11.5 us

profile of v4, /device:TPU:0, one launch (start us, length us, event | category | flops | bytes accessed | tf_op | source)
XLA Modules:
  0.0 235.8 jit_solution(6939009220176093859)
XLA Ops:
  0.7 1.0 convolution_minimum_fusion.4
  1.7 0.3 convolution_minimum_fusion.3
  2.0 0.3 convolution_minimum_fusion.2
  2.2 0.3 convolution_minimum_fusion.1
  2.5 0.3 convolution_minimum_fusion
  2.7 0.3 fusion.5
  3.0 1.7 pad_maximum_fusion.mine
  4.8 0.8 broadcast_in_dim.18
  5.6 155.6 %shard_map.121 = (bf16[4,2,128,128]{3,2,1,0:T(8,128)(2,1)}, bf16[4,2,2,2,2,2,2,16,128]{8,7,6,5,4,3,2,1,0:T(8,128)(2,1)}) custom-call(s32[4]{0:T(128)} %lengths.3, bf16[4,2,144,128]{3,2,1,0:T(8,128)(2,1)} %pad_maximum_fusion.mine, bf16[4,640,8,128]{3,2,1,0:T(8,128)(2,1)} %k.3, bf16[4,640,8,128]{3,2,1,0:T(8,128)(2,1)} %v.3, f32[1024,64]{1,0:T(8,128)} %bitcast.21), custom_call_target="tpu_custom_call" | custom-call | flops 10737418240 | bytes 20971520 | tf_op jit(solution)/shard_map/pallas_call | solution.py:584
  161.2 1.0 copy.13
  162.3 61.3 %shard_map.122 = bf16[256,512]{1,0:T(8,128)(2,1)S(1)} custom-call(bf16[4,2,128,128]{3,2,1,0:T(8,128)(2,1)S(1)} %bitcast.19, bf16[16384,512]{1,0:T(8,128)(2,1)} %weight.1), custom_call_target="tpu_custom_call" | custom-call | tf_op jit(solution)/shard_map/pallas_call | solution.py:285
  223.6 11.5 %shard_map.123 = (bf16[4,640,8,128]{3,2,1,0:T(8,128)(2,1)}, bf16[4,640,8,128]{3,2,1,0:T(8,128)(2,1)}) custom-call(s32[1]{0:T(128)} %bitcast.5.where, s32[4]{0:T(128)} %lengths.3, s32[4,8]{1,0:T(4,128)} %accepted.1, s32[4]{0:T(128)} %count.1, bf16[4,640,8,128]{3,2,1,0:T(8,128)(2,1)} %k.3, bf16[4,640,8,128]{3,2,1,0:T(8,128)(2,1)} %v.3, ...), custom_call_target="tpu_custom_call" | custom-call | tf_op jit(solution)/shard_map/pallas_call | solution.py:639
  235.1 0.7 copy.15
  (2 shorter events, 0.0 us)
